TPU v7x, 32 devices: a whole 2x2x4 slice. The times are simulated.
32 devices in a mesh: dp: 8 (over z, core), ctx: 4 (over y, x).
Axes of the slice: x: 2, y: 2, z: 4, core: 2. Of those that a mesh axis runs over, the one named last changes fastest.
Arguments:
- query: bfloat16 [8, 512, 1024], P('dp', 'ctx'), may hold values from -5 to 5
- key: bfloat16 [8, 512, 512], P('dp', 'ctx'), may hold values from -5 to 5
- value: bfloat16 [8, 512, 512], P('dp', 'ctx'), may hold values from -12 to 12
- out_weight: bfloat16 [1024, 2304], P('dp')
- post_gain: float32 [2304], replicated, may hold values from 0.25 to 4
- grad_out: bfloat16 [8, 512, 2304], P('dp', 'ctx'), may hold values from -6 to 6
- block_lists: int32 [8, 4, 3], P('dp', 'ctx'), may hold values from -1 to 2, as said below
Outputs:
- grad_query: bfloat16 [8, 512, 1024], P('dp', 'ctx')
- grad_key: bfloat16 [8, 512, 512], P('dp', 'ctx')
- grad_value: bfloat16 [8, 512, 512], P('dp', 'ctx')
- grad_wo: float32 [1024, 2304], P('dp')
- grad_gain: float32 [2304], replicated
Inputs may be any that keep to these rules, and one draw needn't show every extreme that they name: `block_lists`: row b of each sequence holds, in its first min(3, b) slots, different block numbers below b, one of which is b - 1 when b >= 1, and -1 in its other slots.
All inputs are finite; a program needn't handle non-finite values.
Results may differ from a plain program's by a relative error of at most 0.02.
Values may be sent and summed in bfloat16 or wider, within the bound.
A program may use at most 64 MiB of HBM per device.

v0:
```python
import functools
import jax
import jax.numpy as jnp
from jax import lax
from jax.experimental import pallas as pl
from jax.experimental.pallas import tpu as pltpu
from jax.sharding import PartitionSpec as P

HD = 256
HQ = 4
HK = 2
BLK = 128
TOPK = 3
LANE = 128
SCALE = 0.0625
NEGATIVE = -1e30
EPSILON = 1e-06
MESH = pl.DeviceIdType.MESH
F32 = jnp.float32
BF16 = jnp.bfloat16


def dot(a, b, dims):
    return lax.dot_general(a, b, (dims, ((), ())), preferred_element_type=F32)


NN = ((1,), (0,))
NT = ((1,), (1,))
TN = ((0,), (0,))


def kernel(
    n, ndp, q, k, v, w, gain, go, bl,
    dq_o, dk_o, dv_o, wo_o, gain_o,
    kbuf, vbuf, wc, goc, hall, probs, mixed, gm, stat, ghs, ghr, gho, gwf, gws, gwr, zs, zr,
    dkf, dvf, dks, dvs, dkr, dvr, wog, gp, gpr, gz, gg,
    kv_s, kv_r, w_s, w_r, wp_s, wp_r, go_s, go_r, h_s, h_r, st_s, st_r, gh_s, gh_r,
    gw_s, gw_r, z_s, z_r, d_s, d_r, wo_s, wo_r, gn_s, gn_r, gg_s, gg_r,
):
    d = lax.axis_index("dp")
    me = lax.axis_index("ctx")
    core = lax.rem(d, 2)
    z = d // 2
    nz = ndp // 2
    partner = d + 1 - 2 * core
    width = w.shape[1]
    square = n == 4
    tiles = width // LANE
    wt = -(-tiles // n)
    win = wt * LANE
    rows = w.shape[0]
    keys = n * BLK
    seqs = float(ndp)

    def start_of(c):
        if isinstance(c, int):
            return min(tiles * c // n, tiles - wt)
        return jnp.minimum(tiles * c // n, tiles - wt)

    def window(c):
        return pl.ds(pl.multiple_of(start_of(c) * LANE, LANE), win)

    def blk(b):
        return pl.ds(pl.multiple_of(b * BLK, BLK), BLK)

    def wrows(b):
        return pl.ds(pl.multiple_of(b * rows, rows), rows)

    def across(i):
        return [me, me + 1 - 2 * lax.rem(me, 2), me + 2 - 4 * (me // 2), 3 - me][i]

    def ahead(i):
        return across(i) if square else lax.rem(me + i, n)

    def behind(i):
        return across(i) if square else lax.rem(me + n - i, n)

    def zpeer(i):
        return lax.rem(z + i, nz) * 2 + core

    def zbehind(i):
        return lax.rem(z + nz - i, nz)

    def copy(src, dst, ss, rs, dev):
        return pltpu.make_async_remote_copy(
            src_ref=src, dst_ref=dst, send_sem=ss, recv_sem=rs, device_id=dev, device_id_type=MESH
        )

    barrier = pltpu.get_barrier_semaphore()
    for i in range(1, n):
        pl.semaphore_signal(barrier, inc=1, device_id=(d, ahead(i)), device_id_type=MESH)
    for i in range(1, nz):
        pl.semaphore_signal(barrier, inc=1, device_id=(zpeer(i), me), device_id_type=MESH)
    pl.semaphore_signal(barrier, inc=1, device_id=(partner, me), device_id_type=MESH)
    pl.semaphore_wait(barrier, n + nz - 1)

    def kv_copies(i, block, dev):
        return [
            copy(k, kbuf.at[blk(block), :], kv_s.at[0, i], kv_r.at[0, i], (d, dev)),
            copy(v, vbuf.at[blk(block), :], kv_s.at[1, i], kv_r.at[1, i], (d, dev)),
        ]

    def kv_part(half, block, slot, to, own):
        held = (vbuf, kbuf)[half].at[block * BLK : (block + 1) * BLK, :]
        src = (v, k)[half] if own else held
        return copy(src, held, kv_s.at[half, slot], kv_r.at[half, slot], (d, to))

    kv_first = {
        0: [(0, 0, 1, 1), (1, 0, 2, 2), (0, 0, 2, 2), (1, 0, 1, 1)],
        1: [(0, 1, 2, 3), (1, 1, 2, 3)],
        2: [(1, 2, 1, 3), (0, 2, 1, 3)],
        3: [],
    }
    kv_then = {
        0: [],
        1: [(0, 0, 1, (3, 3)), (1, 0, 1, None)],
        2: [(1, 0, 2, (3, 3)), (0, 0, 2, None), (0, 1, 1, None), (1, 1, 1, None)],
        3: [
            (0, 1, 2, (1, 2)), (1, 1, 2, (1, 2)), (0, 2, 1, None), (1, 2, 1, None),
            (0, 0, 3, None), (1, 0, 3, None),
        ],
    }
    if square:
        for r in range(n):
            @pl.when(me == r)
            def _(r=r):
                for half, block, slot, to in kv_first[r]:
                    kv_part(half, block, slot, to, True).start()
    else:
        for i in range(1, n):
            @pl.when(ahead(i) > me)
            def _(i=i):
                for c in kv_copies(i, me, ahead(i)):
                    c.start()

    def w_copy(i):
        return copy(w.at[:, window(me)], wc.at[wrows(d), :], w_s.at[i], w_r.at[i], (zpeer(i), me))

    def w_arrived(i):
        there = wc.at[wrows(zbehind(i) * 2 + core), :]
        return copy(there, there, w_s.at[i], w_r.at[i], (zpeer(i), me))

    def w_relay(i):
        there = wc.at[wrows(zbehind(i) * 2 + core), :]
        src = w.at[:, window(me)] if i == 0 else there
        return copy(src, there, wp_s.at[i], wp_r.at[i], (partner, me))

    def w_relayed(i):
        there = wc.at[wrows(zbehind(i) * 2 + 1 - core), :]
        return copy(there, there, wp_s.at[i], wp_r.at[i], (partner, me))

    for i in range(1, nz):
        w_copy(i).start()
    w_relay(0).start()
    wc[wrows(d), :] = w[:, window(me)]
    kbuf[blk(me), :] = k[...]
    vbuf[blk(me), :] = v[...]
    goc[blk(me), :] = go[:, window(me)]
    for u in range(1, n):
        @pl.when(u > me)
        def _(u=u):
            kbuf[u * BLK : (u + 1) * BLK, :] = jnp.zeros((BLK, kbuf.shape[1]), BF16)
            vbuf[u * BLK : (u + 1) * BLK, :] = jnp.zeros((BLK, vbuf.shape[1]), BF16)

    if square:
        for r in range(n):
            @pl.when(me == r)
            def _(r=r):
                for half, block, slot, relay in kv_then[r]:
                    kv_part(half, block, slot, r - 1 if r else 1, False).wait_recv()
                    if relay:
                        kv_part(half, block, relay[0], relay[1], False).start()
                for half, block, slot, to in kv_first[r]:
                    kv_part(half, block, slot, to, True).wait_send()
                for half, block, slot, relay in kv_then[r]:
                    if relay:
                        kv_part(half, block, relay[0], relay[1], False).wait_send()
    else:
        for i in range(1, n):
            @pl.when(behind(i) < me)
            def _(i=i):
                for c in kv_copies(i, behind(i), ahead(i)):
                    c.wait_recv()

    def go_copy(i, block):
        return copy(
            go.at[:, window(ahead(i))], goc.at[blk(block), :], go_s.at[i], go_r.at[i], (d, ahead(i))
        )

    for i in range(1, n):
        go_copy(i, me).start()

    qpos = lax.rem(lax.broadcasted_iota(jnp.int32, (2 * BLK, keys), 0), BLK)
    kpos = lax.broadcasted_iota(jnp.int32, (2 * BLK, keys), 1)
    allowed = (kpos <= qpos + me * BLK) & (kpos >= me * BLK)
    for s in range(TOPK):
        first = bl[0, s] * BLK
        allowed = allowed | ((kpos >= first) & (kpos < first + BLK) & (kpos >= 0))

    def pair(x, j):
        return jnp.concatenate(
            [x[:, 2 * j * HD : (2 * j + 1) * HD], x[:, (2 * j + 1) * HD : (2 * j + 2) * HD]], axis=0
        )

    def h_copy(j, i, block):
        ref = hall.at[blk(block), pl.ds(j * 2 * HD, 2 * HD)]
        return copy(ref, ref, h_s.at[j, i], h_r.at[j, i], (d, ahead(i)))

    def relayed(part):
        def send(half, hop, block):
            to = hop if hop < 3 else 2 - half
            return part(half, hop, to, block)

        return send

    def relay_on(send):
        for half in range(2):
            send(half, half + 1, across(half + 1)).wait_recv()
            send(half, 3, across(half + 1)).start()

    def relay_end(send):
        for half in range(2):
            send(half, 2 - half, across(2 - half)).wait_recv()
            send(half, 3, across(3)).wait_recv()

    def relay_drain(send):
        for half in range(2):
            for hop in (1, 2):
                send(half, hop, me).wait_send()
            send(half, 3, across(half + 1)).wait_send()

    def h_part(half, slot, to, block):
        ref = hall.at[blk(block), pl.ds(half * 2 * HD, 2 * HD)]
        return copy(ref, ref, h_s.at[half, slot], h_r.at[half, slot], (d, across(to)))

    def wo_part(half, slot, to, block):
        ref = wog.at[block, pl.ds(half * (rows // 2), rows // 2), :]
        return copy(ref, ref, wo_s.at[half, slot], wo_r.at[half, slot], (d, across(to)))

    h_send, wo_send = relayed(h_part), relayed(wo_part)

    for j in range(HK):
        logits = dot(pair(q, j), kbuf[:, j * HD : (j + 1) * HD], NT) * SCALE
        logits = jnp.where(allowed, logits, NEGATIVE)
        e = jnp.exp(logits - jnp.max(logits, axis=-1, keepdims=True))
        p = e / jnp.sum(e, axis=-1, keepdims=True)
        probs[j] = p
        out = dot(p.astype(BF16), vbuf[:, j * HD : (j + 1) * HD], NN).astype(BF16)
        hall[blk(me), 2 * j * HD : (2 * j + 1) * HD] = out[:BLK]
        hall[blk(me), (2 * j + 1) * HD : (2 * j + 2) * HD] = out[BLK:]
        if square:
            h_send(j, j + 1, me).start()
        else:
            for i in range(1, n):
                h_copy(j, i, me).start()
    if square:
        h_send(0, 2, me).start()
        h_send(1, 1, me).start()
        relay_on(h_send)

    for i in range(1, nz):
        w_arrived(i).wait_recv()
        w_relay(i).start()
    for i in range(nz):
        w_relayed(i).wait_recv()

    col = lax.broadcasted_iota(jnp.int32, (1, win), 1) // LANE + start_of(me)
    live = (col >= tiles * me // n) & (col < tiles * (me + 1) // n)
    gain_win = gain[window(me)].reshape(1, win)
    lane = lax.broadcasted_iota(jnp.int32, (BLK, LANE), 1)
    for i in range(n):
        b = behind(i)
        if i:
            if not square:
                for j in range(HK):
                    h_copy(j, i, b).wait_recv()
            elif i < 3:
                h_send(2 - i, i, b).wait_recv()
            else:
                h_send(0, 3, b).wait_recv()
                h_send(1, 3, b).wait_recv()
            go_copy(i, b).wait_recv()
        part = jnp.where(live, dot(hall[blk(b), :], wc[...], NN), 0.0)
        mixed[blk(b), :] = part
        scaled = goc[blk(b), :].astype(F32) * gain_win
        energy = jnp.sum(part * part, axis=-1, keepdims=True)
        cross = jnp.sum(scaled * part, axis=-1, keepdims=True)
        both = jnp.where(lane == 0, energy, jnp.where(lane == 1, cross, 0.0))
        stat[me, b] = jnp.transpose(both)[:8]

    def st_copy(i, slot):
        return copy(stat.at[slot], stat.at[slot], st_s.at[i], st_r.at[i], (d, ahead(i)))

    for i in range(1, n):
        st_copy(i, me).start()
    for i in range(1, n):
        st_copy(i, behind(i)).wait_recv()

    def gh_copy(i):
        return copy(ghs.at[i], ghr.at[i], gh_s.at[i], gh_r.at[i], (d, ahead(i)))

    gain_part = jnp.zeros((1, win), F32)
    for step in range(n):
        i = (step + 1) % n
        b = ahead(i)
        total = stat[0, b]
        for c in range(1, n):
            total = total + stat[c, b]
        turned = jnp.transpose(jnp.concatenate([total] * (LANE // 8), axis=0))
        inv = lax.rsqrt(turned[:, 0:1] / width + EPSILON)
        cross = turned[:, 1:2] / width
        part = mixed[blk(b), :]
        upstream = goc[blk(b), :].astype(F32)
        grad = inv * (upstream * gain_win - part * (inv * inv * cross))
        grad = jnp.where(live, grad, 0.0).astype(BF16)
        gm[blk(b), :] = grad
        back = dot(grad, wc[...], NT)
        if i:
            ghs[i] = back.astype(BF16)
            gh_copy(i).start()
        else:
            gho[...] = back
        gain_part = gain_part + jnp.sum(upstream * part * inv, axis=0, keepdims=True)
    gp[...] = jnp.broadcast_to(gain_part, (8, win))

    def gp_copy():
        return copy(gp, gpr, gn_s.at[0], gn_r.at[0], (partner, me))

    gp_copy().start()

    for j in range(HQ):
        both = dot(hall[:, j * HD : (j + 1) * HD], gm[...], TN)
        gwf[j * HD : (j + 1) * HD, :] = both
        gws[j * HD : (j + 1) * HD, :] = both.astype(BF16)

    def gw_copy(zz):
        return copy(
            gws.at[wrows(zz * 2 + 1 - core), :], gwr.at[zz], gw_s.at[zz], gw_r.at[zz], (partner, me)
        )

    def z_copy(i):
        return copy(zs.at[i], zr.at[i], z_s.at[i], z_r.at[i], (zpeer(i), me))

    def gz_copy(i, slot):
        return copy(gz.at[slot], gz.at[slot], gn_s.at[i], gn_r.at[i], (zpeer(i), me))

    for zz in range(nz):
        gw_copy(zz).start()
    gp_copy().wait_recv()
    gz[z] = gp[...] + gpr[...]
    for zz in range(nz):
        gw_copy(zz).wait_recv()
    for i in range(1, nz):
        zz = lax.rem(z + i, nz)
        zs[i] = (gwf[wrows(zz * 2 + core), :] + gwr[zz].astype(F32)).astype(BF16)
        z_copy(i).start()
        gz_copy(i, z).start()

    back = gho[...]
    for i in range(1, n):
        gh_copy(i).wait_recv()
        back = back + ghr[i].astype(F32)
    back = back.astype(BF16)
    held = hall[blk(me), :]
    for j in range(HK):
        gj = pair(back, j)
        oj = pair(held, j)
        delta = jnp.sum(gj.astype(F32) * oj.astype(F32), axis=-1, keepdims=True)
        span = slice(j * HD, (j + 1) * HD)
        gprob = dot(gj, vbuf[:, span], NT)
        p = probs[j]
        ds = (p * (gprob - delta) * SCALE).astype(BF16)
        dv = dot(p.astype(BF16), gj, TN)
        dk = dot(ds, pair(q, j), TN)
        dvf[:, span] = dv
        dkf[:, span] = dk
        dvs[:, span] = dv.astype(BF16)
        dks[:, span] = dk.astype(BF16)
        dq = dot(ds, kbuf[:, span], NN).astype(BF16)
        dq_o[:, 2 * j * HD : (2 * j + 1) * HD] = dq[:BLK]
        dq_o[:, (2 * j + 1) * HD : (2 * j + 2) * HD] = dq[BLK:]

    def d_copies(i):
        dev = (d, behind(i))
        return [
            copy(dks.at[blk(behind(i)), :], dkr.at[i], d_s.at[0, i], d_r.at[0, i], dev),
            copy(dvs.at[blk(behind(i)), :], dvr.at[i], d_s.at[1, i], d_r.at[1, i], dev),
        ]

    for i in range(1, n):
        @pl.when(behind(i) < me)
        def _(i=i):
            for c in d_copies(i):
                c.start()

    total = gwf[wrows(d), :] + gwr[z].astype(F32)
    for i in range(1, nz):
        z_copy(i).wait_recv()
        total = total + zr[i].astype(F32)
        gz_copy(i, zbehind(i)).wait_recv()
    wog[me] = total.astype(BF16)
    small = gz[0]
    for zz in range(1, nz):
        small = small + gz[zz]
    gg[me] = small

    def wo_copy(i, slot):
        return copy(wog.at[slot], wog.at[slot], wo_s.at[0, i], wo_r.at[0, i], (d, ahead(i)))

    def gg_copy(i, slot):
        return copy(gg.at[slot], gg.at[slot], gg_s.at[i], gg_r.at[i], (d, ahead(i)))

    if square:
        for half, hop in ((0, 1), (1, 2), (0, 2), (1, 1)):
            wo_send(half, hop, me).start()
    for i in range(1, n):
        if not square:
            wo_copy(i, me).start()
        gg_copy(i, me).start()
    if square:
        relay_on(wo_send)

    dkf[blk(0), :] = dkf[blk(me), :]
    dvf[blk(0), :] = dvf[blk(me), :]
    for i in range(1, n):
        @pl.when(ahead(i) > me)
        def _(i=i):
            for c in d_copies(i):
                c.wait_recv()
            dkf[blk(0), :] += dkr[i].astype(F32)
            dvf[blk(0), :] += dvr[i].astype(F32)

    dk_o[...] = dkf[blk(0), :].astype(BF16)
    dv_o[...] = dvf[blk(0), :].astype(BF16)

    if square:
        relay_end(wo_send)
    for i in range(1, n):
        if not square:
            wo_copy(i, behind(i)).wait_recv()
        gg_copy(i, behind(i)).wait_recv()
    for c in range(n):
        lo, hi = tiles * c // n, tiles * (c + 1) // n
        at = (lo - start_of(c)) * LANE
        span = slice(lo * LANE, hi * LANE)
        wo_o[:, span] = wog[c, :, at : at + (hi - lo) * LANE]
        gain_o[span] = gg[c, 0, at : at + (hi - lo) * LANE] / seqs

    if square:
        relay_drain(h_send)
        relay_drain(wo_send)
    for i in range(1, n):
        @pl.when(behind(i) < me)
        def _(i=i):
            for c in d_copies(i):
                c.wait_send()

        if not square:
            @pl.when(ahead(i) > me)
            def _(i=i):
                for c in kv_copies(i, me, ahead(i)):
                    c.wait_send()

            for j in range(HK):
                h_copy(j, i, me).wait_send()
            wo_copy(i, me).wait_send()
        go_copy(i, me).wait_send()
        st_copy(i, me).wait_send()
        gh_copy(i).wait_send()
        gg_copy(i, me).wait_send()
    for i in range(1, nz):
        w_copy(i).wait_send()
        z_copy(i).wait_send()
        gz_copy(i, z).wait_send()
    for i in range(nz):
        w_relay(i).wait_send()
        gw_copy(i).wait_send()
    gp_copy().wait_send()


def per_device(n, ndp, query, key, value, out_weight, post_gain, grad_out, block_lists):
    width = out_weight.shape[1]
    rows = out_weight.shape[0]
    tiles = width // LANE
    win = -(-tiles // n) * LANE
    keys = n * BLK
    nz = ndp // 2
    qw, kw = HQ * HD, HK * HD
    vm = pl.BlockSpec(memory_space=pltpu.VMEM)
    dma = pltpu.SemaphoreType.DMA
    dq, dk, dv, wo, gain = pl.pallas_call(
        functools.partial(kernel, n, ndp),
        out_shape=(
            jax.ShapeDtypeStruct((BLK, qw), BF16),
            jax.ShapeDtypeStruct((BLK, kw), BF16),
            jax.ShapeDtypeStruct((BLK, kw), BF16),
            jax.ShapeDtypeStruct((rows, width), BF16),
            jax.ShapeDtypeStruct((width,), F32),
        ),
        in_specs=[vm] * 6 + [pl.BlockSpec(memory_space=pltpu.SMEM)],
        out_specs=[vm] * 5,
        scratch_shapes=[
            pltpu.VMEM((keys, kw), BF16),
            pltpu.VMEM((keys, kw), BF16),
            pltpu.VMEM((qw, win), BF16),
            pltpu.VMEM((keys, win), BF16),
            pltpu.VMEM((keys, qw), BF16),
            pltpu.VMEM((HK, 2 * BLK, keys), F32),
            pltpu.VMEM((keys, win), F32),
            pltpu.VMEM((keys, win), BF16),
            pltpu.VMEM((n, n, 8, LANE), F32),
            pltpu.VMEM((n, BLK, qw), BF16),
            pltpu.VMEM((n, BLK, qw), BF16),
            pltpu.VMEM((BLK, qw), F32),
            pltpu.VMEM((qw, win), F32),
            pltpu.VMEM((qw, win), BF16),
            pltpu.VMEM((nz, rows, win), BF16),
            pltpu.VMEM((nz, rows, win), BF16),
            pltpu.VMEM((nz, rows, win), BF16),
            pltpu.VMEM((keys, kw), F32),
            pltpu.VMEM((keys, kw), F32),
            pltpu.VMEM((keys, kw), BF16),
            pltpu.VMEM((keys, kw), BF16),
            pltpu.VMEM((n, BLK, kw), BF16),
            pltpu.VMEM((n, BLK, kw), BF16),
            pltpu.VMEM((n, rows, win), BF16),
            pltpu.VMEM((8, win), F32),
            pltpu.VMEM((8, win), F32),
            pltpu.VMEM((nz, 8, win), F32),
            pltpu.VMEM((n, 8, win), F32),
            dma((2, n)), dma((2, n)), dma((nz,)), dma((nz,)), dma((nz,)), dma((nz,)),
            dma((n,)), dma((n,)), dma((HK, n)), dma((HK, n)), dma((n,)), dma((n,)),
            dma((n,)), dma((n,)), dma((nz,)), dma((nz,)), dma((nz,)), dma((nz,)),
            dma((2, n)), dma((2, n)), dma((2, n)), dma((2, n)), dma((nz,)), dma((nz,)), dma((n,)), dma((n,)),
        ],
        compiler_params=pltpu.CompilerParams(
            collective_id=0, has_side_effects=True, vmem_limit_bytes=56 * 2**20
        ),
        cost_estimate=pl.CostEstimate(flops=4 * 10**9, bytes_accessed=6 * 10**6, transcendentals=262144),
    )(
        query[0], key[0], value[0], out_weight, post_gain, grad_out[0], block_lists[0],
    )
    return (dq[None], dk[None], dv[None], wo.astype(F32) / ndp, gain)


def solution(mesh):
    n, ndp = mesh.shape["ctx"], mesh.shape["dp"]
    seq = P("dp", "ctx", None)
    return jax.shard_map(
        functools.partial(per_device, n, ndp),
        mesh=mesh,
        in_specs=(seq, seq, seq, P("dp", None), P(), seq, seq),
        out_specs=(seq, seq, seq, P("dp", None), P()),
        check_vma=False,
    )
```

profile of v0, /device:TPU:0, one launch (start us, length us, event | category | flops | bytes accessed | tf_op | source)
XLA Modules:
  0.0 80.8 jit_solution(13455224465089310675)
XLA Ops:
  0.6 75.3 %shard_map.110 = (bf16[128,1024]{1,0:T(8,128)(2,1)}, bf16[128,512]{1,0:T(8,128)(2,1)}, bf16[128,512]{1,0:T(8,128)(2,1)}, bf16[128,2304]{1,0:T(8,128)(2,1)}, f32[2304]{0:T(1024)}) custom-call(bf16[128,1024]{1,0:T(8,128)(2,1)} %bitcast.12, bf16[128,512]{1,0:T(8,128)(2,1)} %bitcast.13, bf16[128,512]{1,0:T(8,128)(2,1)} %bitcast.14, bf16[128,2304]{1,0:T(8,128)(2,1)} %w.1, ...), custom_call_target="tpu_custom_call" | custom-call | flops 4000000000 | bytes 6000000 | tf_op jit(solution)/shard_map/pallas_call | solution.py:491
  75.9 0.0 copy-start
  75.9 0.0 copy-start.2
  75.9 0.0 copy-start.1
  75.9 0.0 copy-start.3
  76.0 2.2 %convert_multiply_fusion = f32[128,2304]{1,0:T(8,128)} fusion(bf16[128,2304]{1,0:T(8,128)(2,1)} %get-tuple-element.13), kind=kLoop, calls=%fused_computation | loop fusion | flops 589824 | bytes 1769472 | tf_op jit(solution)/shard_map/div | solution.py:543
  78.2 0.0 copy-done
  78.2 0.7 copy.16
  78.9 0.0 copy-done.2
  78.9 0.7 copy.17
  79.5 0.0 copy-done.1
  79.5 0.7 copy.18
  80.2 0.0 copy-done.3
  80.2 0.6 copy.19
Async XLA Ops:
  75.9 2.2 %copy-start = (bf16[128,1024]{1,0:T(8,128)(2,1)S(1)}, bf16[128,1024]{1,0:T(8,128)(2,1)}, u32[]{:S(2)}) copy-start(bf16[128,1024]{1,0:T(8,128)(2,1)} %get-tuple-element.10) | copy-start | bytes 786436
  75.9 2.9 %copy-start.2 = (bf16[128,512]{1,0:T(8,128)(2,1)S(1)}, bf16[128,512]{1,0:T(8,128)(2,1)}, u32[]{:S(2)}) copy-start(bf16[128,512]{1,0:T(8,128)(2,1)} %get-tuple-element.11) | copy-start | bytes 393220
  75.9 3.6 %copy-start.1 = (bf16[128,512]{1,0:T(8,128)(2,1)S(1)}, bf16[128,512]{1,0:T(8,128)(2,1)}, u32[]{:S(2)}) copy-start(bf16[128,512]{1,0:T(8,128)(2,1)} %get-tuple-element.12) | copy-start | bytes 393220
  75.9 4.2 %copy-start.3 = (f32[2304]{0:T(1024)S(1)}, f32[2304]{0:T(1024)}, u32[]{:S(2)}) copy-start(f32[2304]{0:T(1024)} %get-tuple-element.24) | copy-start | bytes 27652
where the time goes:
time: 81 us; the launch traced here: 80.8 us
  Pallas kernels  75.3 us (93%)
  local copies, waits for them, and re-layouts  2.63 us (3%)
  other arithmetic  2.21 us (3%)
    pallas_call x1, Pallas kernels, per_device(): pl.pallas_call(functools.partial(kernel, n, ndp), out_shape=(jax.ShapeDty...  75.3 us
    unnamed x12, local copies, waits for them, and re-layouts  2.63 us
    div x1, other arithmetic, per_device(): return (dq[None], dk[None], dv[None], wo.astype(F32) / ndp, gain)  2.21 us

commit v1 on v0

--- a/solution.py
+++ b/solution.py
@@ -187,8 +187,6 @@
             go.at[:, window(ahead(i))], goc.at[blk(block), :], go_s.at[i], go_r.at[i], (d, ahead(i))
         )
 
-    for i in range(1, n):
-        go_copy(i, me).start()
 
     qpos = lax.rem(lax.broadcasted_iota(jnp.int32, (2 * BLK, keys), 0), BLK)
     kpos = lax.broadcasted_iota(jnp.int32, (2 * BLK, keys), 1)
@@ -257,6 +255,8 @@
         h_send(0, 2, me).start()
         h_send(1, 1, me).start()
         relay_on(h_send)
+    for i in range(1, n):
+        go_copy(i, me).start()
 
     for i in range(1, nz):
         w_arrived(i).wait_recv()

time: 81 us -> 77 us (0.951)
  Pallas kernels: 75.3 us -> 71.4 us
    pallas_call x1, Pallas kernels: 75.3 us -> 71.4 us  [per_device(): pl.pallas_call(functools.partial(kernel, n, ndp), out_shape=(jax.ShapeDty...]
where the time goes in v1:
time: 77 us; the launch traced here: 76.9 us
  Pallas kernels  71.4 us (93%)
  local copies, waits for them, and re-layouts  2.63 us (3%)
  other arithmetic  2.21 us (3%)
    pallas_call x1, Pallas kernels, per_device(): pl.pallas_call(functools.partial(kernel, n, ndp), out_shape=(jax.ShapeDty...  71.4 us
    unnamed x12, local copies, waits for them, and re-layouts  2.63 us
    div x1, other arithmetic, per_device(): return (dq[None], dk[None], dv[None], wo.astype(F32) / ndp, gain)  2.21 us

profile of v1, /device:TPU:0, one launch (start us, length us, event | category | flops | bytes accessed | tf_op | source)
XLA Modules:
  0.0 76.9 jit_solution(6065482911252951722)
XLA Ops:
  0.6 71.4 %shard_map.110 = (bf16[128,1024]{1,0:T(8,128)(2,1)}, bf16[128,512]{1,0:T(8,128)(2,1)}, bf16[128,512]{1,0:T(8,128)(2,1)}, bf16[128,2304]{1,0:T(8,128)(2,1)}, f32[2304]{0:T(1024)}) custom-call(bf16[128,1024]{1,0:T(8,128)(2,1)} %bitcast.12, bf16[128,512]{1,0:T(8,128)(2,1)} %bitcast.13, bf16[128,512]{1,0:T(8,128)(2,1)} %bitcast.14, bf16[128,2304]{1,0:T(8,128)(2,1)} %w.1, ...), custom_call_target="tpu_custom_call" | custom-call | flops 4000000000 | bytes 6000000 | tf_op jit(solution)/shard_map/pallas_call | solution.py:491
  72.0 0.0 copy-start
  72.0 0.0 copy-start.2
  72.0 0.0 copy-start.1
  72.0 0.0 copy-start.3
  72.0 2.2 %convert_multiply_fusion = f32[128,2304]{1,0:T(8,128)} fusion(bf16[128,2304]{1,0:T(8,128)(2,1)} %get-tuple-element.13), kind=kLoop, calls=%fused_computation | loop fusion | flops 589824 | bytes 1769472 | tf_op jit(solution)/shard_map/div | solution.py:543
  74.2 0.0 copy-done
  74.2 0.7 copy.16
  75.0 0.0 copy-done.2
  75.0 0.7 copy.17
  75.6 0.0 copy-done.1
  75.6 0.7 copy.18
  76.3 0.0 copy-done.3
  76.3 0.6 copy.19
Async XLA Ops:
  72.0 2.2 %copy-start = (bf16[128,1024]{1,0:T(8,128)(2,1)S(1)}, bf16[128,1024]{1,0:T(8,128)(2,1)}, u32[]{:S(2)}) copy-start(bf16[128,1024]{1,0:T(8,128)(2,1)} %get-tuple-element.10) | copy-start | bytes 786436
  72.0 2.9 %copy-start.2 = (bf16[128,512]{1,0:T(8,128)(2,1)S(1)}, bf16[128,512]{1,0:T(8,128)(2,1)}, u32[]{:S(2)}) copy-start(bf16[128,512]{1,0:T(8,128)(2,1)} %get-tuple-element.11) | copy-start | bytes 393220
  72.0 3.6 %copy-start.1 = (bf16[128,512]{1,0:T(8,128)(2,1)S(1)}, bf16[128,512]{1,0:T(8,128)(2,1)}, u32[]{:S(2)}) copy-start(bf16[128,512]{1,0:T(8,128)(2,1)} %get-tuple-element.12) | copy-start | bytes 393220
  72.0 4.2 %copy-start.3 = (f32[2304]{0:T(1024)S(1)}, f32[2304]{0:T(1024)}, u32[]{:S(2)}) copy-start(f32[2304]{0:T(1024)} %get-tuple-element.24) | copy-start | bytes 27652
